TPU v7x, 256 devices: a whole 4x4x8 slice. The times are simulated.
256 devices in a mesh: section: 8 (over x, core), vocab: 32 (over y, z).
Axes of the slice: x: 4, y: 4, z: 8, core: 2. Of those that a mesh axis runs over, the one named last changes fastest.
Arguments:
- hidden: bfloat16 [2048, 8192], P('section', 'vocab'), may hold values from -1000 to 1000
- norm_gain: float32 [8192], P('vocab'), may hold values from 0.5 to 1.5
- head_weight: bfloat16 [8192, 98304], P(None, ('section', 'vocab')), may hold values from -5 to 5
- exit_mask: int32 [2048], replicated, may hold values from 0 to 1, as said below
- targets: int32 [2048], replicated, may hold values from 0 to 98303
- section_weight: float32 [8], replicated, may hold values from 8 to 24
Outputs:
- mean_loss: float32 [], replicated
- d_hidden: bfloat16 [2048, 8192], P('section', 'vocab')
- d_gain: float32 [8192], P('vocab')
- d_head: bfloat16 [8192, 98304], P(None, ('section', 'vocab'))
Inputs may be any that keep to these rules, and one draw needn't show every extreme that they name: `exit_mask`: exactly 384 ones in all; at most 96 ones among the 256 tokens of one section group, and exactly 96 in some section group.
All inputs are finite; a program needn't handle non-finite values.
Results may differ from a plain program's by a relative error of at most 0.027.
Values may be sent and summed in bfloat16 or wider, within the bound.
No kernel may reach another device: no remote copies, remote signals or barrier semaphores. Data moves between devices by JAX's collectives and lax.ppermute only.
A program may use at most 128 MiB of HBM per device.

v0:
```python
import jax
import jax.numpy as jnp
from jax import lax
from jax.sharding import PartitionSpec as P

D = 8192
CAP = 96
EXIT_MEAN = 48
epsilon = 1e-05


def body(hidden, norm_gain, head_weight, exit_mask, targets, section_weight):
    section_count = lax.axis_size("section")
    vocab_count = lax.axis_size("vocab")
    section_index = lax.axis_index("section")
    vocab_index = lax.axis_index("vocab")
    token_count = hidden.shape[0]
    vocab_width = head_weight.shape[1]
    exit_total = EXIT_MEAN * section_count
    mask_grid = exit_mask.reshape(section_count, token_count)
    rank_grid = jnp.cumsum(mask_grid, axis=1) - 1
    slot_iota = jnp.arange(CAP, dtype=jnp.int32)
    token_iota = jnp.arange(token_count, dtype=jnp.int32)
    slot_hit = (rank_grid[:, None, :] == slot_iota[None, :, None]) & (mask_grid[:, None, :] == 1)
    own_hit = lax.dynamic_index_in_dim(slot_hit, section_index, 0, keepdims=False)
    rows_own = jnp.dot(own_hit.astype(jnp.bfloat16), hidden, preferred_element_type=jnp.float32)
    squares = lax.psum(jnp.sum(rows_own * rows_own, axis=1), "vocab")
    inverse = lax.rsqrt(squares / D + epsilon)
    normed_own = (rows_own * inverse[:, None] * norm_gain[None, :]).astype(jnp.bfloat16)
    section_rows = lax.all_gather(normed_own, "section", axis=0, tiled=True)
    local_place = jnp.sum(jnp.where(slot_hit, token_iota[None, None, :], 0), axis=2)
    section_start = jnp.arange(section_count, dtype=jnp.int32)[:, None] * token_count
    positions = (local_place + section_start).reshape(-1)
    live_rows = jnp.any(slot_hit, axis=2).reshape(-1).astype(jnp.float32)
    full_rows = lax.all_gather(section_rows, "vocab", axis=1, tiled=True)
    labels = targets[positions]
    weights = section_weight[positions // token_count] * live_rows
    logits = jnp.dot(full_rows, head_weight, preferred_element_type=jnp.float32)
    vocab_start = (section_index * vocab_count + vocab_index) * vocab_width
    column = jnp.arange(vocab_width, dtype=jnp.int32) + vocab_start
    onehot = (column[None, :] == labels[:, None]).astype(jnp.float32)
    picked_part = jnp.sum(logits * onehot, axis=1)
    local_peak = jnp.max(logits, axis=1)
    row_peak = lax.pmax(local_peak, ("section", "vocab"))
    local_total = jnp.sum(jnp.exp(logits - row_peak[:, None]), axis=1)
    row_total, picked = lax.psum((local_total, picked_part), ("section", "vocab"))
    logsum = row_peak + jnp.log(row_total)
    mean_loss = jnp.sum(live_rows * (logsum - picked)) / exit_total
    softmax_rows = jnp.exp(logits - logsum[:, None])
    dlogits = (weights[:, None] * (softmax_rows - onehot)).astype(jnp.bfloat16)
    d_head = lax.dot_general(
        full_rows, dlogits, (((0,), (0,)), ((), ())), preferred_element_type=jnp.float32
    ).astype(jnp.bfloat16)
    grads_turned = lax.psum_scatter(
        lax.dot_general(
            head_weight, dlogits, (((1,), (1,)), ((), ())), preferred_element_type=jnp.float32
        ).astype(jnp.bfloat16),
        "vocab",
        scatter_dimension=0,
        tiled=True,
    )
    own_grads = lax.psum_scatter(grads_turned, "section", scatter_dimension=1, tiled=True).astype(
        jnp.float32
    )
    d_normed = own_grads.T
    scaled = d_normed * norm_gain[None, :]
    inner_dots = lax.psum(jnp.sum(scaled * rows_own, axis=1), "vocab") / D
    d_rows = (
        inverse[:, None] * scaled - rows_own * (inverse * inverse * inverse * inner_dots)[:, None]
    )
    gain_part = jnp.sum(d_normed * rows_own * inverse[:, None], axis=0)
    d_gain = lax.psum(gain_part, "section")
    d_hidden = lax.dot_general(
        own_hit.astype(jnp.float32),
        d_rows,
        (((0,), (0,)), ((), ())),
        precision=lax.Precision.HIGHEST,
        preferred_element_type=jnp.float32,
    ).astype(jnp.bfloat16)
    return (mean_loss, d_hidden, d_gain, d_head)


def solution(mesh):
    placed = (P("section", "vocab"), P("vocab"), P(None, ("section", "vocab")), P(), P(), P())
    return jax.shard_map(
        body,
        mesh=mesh,
        in_specs=placed,
        out_specs=(P(), P("section", "vocab"), P("vocab"), P(None, ("section", "vocab"))),
        check_vma=False,
    )
```

profile of v0, /device:TPU:0, one launch (start us, length us, event | category | flops | bytes accessed | tf_op | source)
XLA Modules:
  0.0 760.4 jit_solution(11784540676493656308)
XLA Ops:
  7.2 0.0 copy-start
  7.2 0.0 copy-start.1
  7.2 0.0 all-gather.2.cloned.1.call-start
  7.2 0.7 broadcast_compare_fusion
  8.0 0.7 copy.11
  8.7 0.6 reduce-window.6
  9.2 0.2 slice_reduce_fusion
  9.5 0.1 add_bitcast_fusion
  9.6 0.3 fusion.5
  9.8 0.0 copy-done
  9.8 0.3 multiply_reduce_fusion
  10.1 76.2 %psum.35 = f32[96]{0:T(128)S(1)} all-reduce(f32[96]{0:T(128)S(1)} %get-tuple-element.25), channel_id=1, replica_groups=mesh['section'=8,'vocab'=32] {'vocab'}, use_global_device_ids=true, to_apply=%region_4.5 | all-reduce | flops 96 | bytes 768 | tf_op jit(solution)/shard_map/psum | solution.py:27
  86.3 0.8 multiply_convert_fusion
  87.1 14.4 %all_gather.6 = bf16[768,256]{1,0:T(8,128)(2,1)} all-gather(bf16[96,256]{1,0:T(8,128)(2,1)S(1)} %multiply_convert_fusion), channel_id=1, replica_groups=mesh['section'=8,'vocab'=32] {'section'}, dimensions={0}, use_global_device_ids=true | all-gather | bytes 442368 | tf_op jit(solution)/shard_map/all_gather | solution.py:30
  101.5 0.0 all-gather.2.cloned.1.call-update
  101.5 0.0 reduce-scatter.3.cloned.1.call-start
  101.5 0.2 select_reduce_fusion
  101.8 0.1 broadcast_add_fusion
  101.9 0.1 add.110
  101.9 0.1 reshape.157
  102.1 0.0 copy-done.1
  102.1 0.0 copy-start.2
  102.1 4.5 gather_fusion
  106.6 0.0 copy-done.2
  106.6 0.7 fusion.30
  107.3 4.4 fusion.23
  111.7 110.2 %all-gather.2.cloned.1.call-done = bf16[768,8192]{1,0:T(8,128)(2,1)} async-done(((bf16[768,256]{1,0:T(8,128)(2,1)}), bf16[768,8192]{1,0:T(8,128)(2,1)}) %all-gather.2.cloned.1.call-update) | async-done | bytes 12582928 | tf_op jit(solution)/shard_map/all_gather | solution.py:35
  221.9 11.3 %fusion.31 = (f32[768]{0:T(1024)S(1)}, f32[768,384]{0,1:T(8,128)S(1)}) fusion(bf16[768,8192]{1,0:T(8,128)(2,1)} %all-gather.2.cloned.1.call-done, bf16[8192,384]{1,0:T(8,128)(2,1)} %param.8), kind=kOutput, calls=%fused_computation.66 | convolution fusion | flops 4832132096 | bytes 20057088 | tf_op jit(solution)/shard_map/dot_general | solution.py:38
  233.2 75.4 %pmax.7 = f32[768]{0:T(1024)S(1)} all-reduce(f32[768]{0:T(1024)S(1)} %get-tuple-element.27), channel_id=1, replica_groups=mesh['section'=8,'vocab'=32] {'section','vocab'}, use_global_device_ids=true, to_apply=%region_6.7 | all-reduce | flops 768 | bytes 6144 | tf_op jit(solution)/shard_map/pmax | solution.py:44
  308.6 0.3 fusion.1
  308.9 72.1 %all-reduce = (f32[768]{0:T(1024)S(1)}, f32[768]{0:T(1024)S(1)}) all-reduce(f32[768]{0:T(1024)S(1)} %get-tuple-element.5, f32[768]{0:T(1024)S(1)} %get-tuple-element.4), channel_id=1, replica_groups=mesh['section'=8,'vocab'=32] {'section','vocab'}, use_global_device_ids=true, to_apply=%region_8.9 | all-reduce | flops 1536 | bytes 12288 | tf_op jit(solution)/shard_map/psum | solution.py:46
  381.0 1.3 select_reduce_fusion.1
  382.3 12.6 %fusion = bf16[8192,768]{0,1:T(8,128)(2,1)} fusion(bf16[8192,384]{1,0:T(8,128)(2,1)} %param.8, f32[768,384]{0,1:T(8,128)S(1)} %get-tuple-element.28, f32[768]{0:T(1024)S(1)} %get-tuple-element.13, f32[768]{0:T(1024)S(1)} %get-tuple-element.16, s32[768]{0:T(1024)S(1)} %gather_fusion, s32[384]{0:T(512)S(1)} %iota_add_fusion), kind=kOutput, calls=%fused_computation.2 | convolution fusion | flops 4839899136 | bytes 20064768 | tf_op jit(solution)/shard_map/dot_general | solution.py:55
  394.9 0.0 reduce-scatter.3.cloned.1.call-update
  394.9 0.2 reduce-scatter.5.cloned.1.call-start
  395.8 231.7 %reduce-scatter.3.cloned.1.call-done = bf16[256,768]{0,1:T(8,128)(2,1)} async-done(((bf16[8192,768]{0,1:T(8,128)(2,1)}), bf16[256,768]{0,1:T(8,128)(2,1)}) %reduce-scatter.3.cloned.1.call-update) | async-done | bytes 393232 | tf_op jit(solution)/shard_map/reduce_scatter | solution.py:54
  627.5 0.0 reduce-scatter.5.cloned.1.call-update
  627.5 0.0 copy-start.3
  627.5 11.7 %convolution_convert_fusion.1 = bf16[8192,384]{1,0:T(8,128)(2,1)} fusion(bf16[768,8192]{1,0:T(8,128)(2,1)} %all-gather.2.cloned.1.call-done, f32[768,384]{0,1:T(8,128)S(1)} %get-tuple-element.28, f32[768]{0:T(1024)S(1)} %get-tuple-element.13, f32[768]{0:T(1024)S(1)} %get-tuple-element.16, s32[768]{0:T(1024)S(1)} %gather_fusion, s32[384]{0:T(512)S(1)} %iota_add_fusion), kind=kOutput, calls=%fused_computation.3 | convolution fusion | flops 4836753408 | bytes 20064768 | tf_op jit(solution)/shard_map/dot_general | solution.py:51
  639.2 22.3 %reduce-scatter.5.cloned.1.call-done = bf16[256,96]{0,1:T(8,128)(2,1)} async-done(((bf16[256,768]{0,1:T(8,128)(2,1)}), bf16[256,96]{0,1:T(8,128)(2,1)}) %reduce-scatter.5.cloned.1.call-update) | async-done | bytes 49168 | tf_op jit(solution)/shard_map/reduce_scatter | solution.py:62
  661.5 0.0 copy-done.3
  661.5 1.0 fusion.12
  662.5 13.7 %psum.39 = f32[256]{0:T(256)} all-reduce(f32[256]{0:T(256)S(1)} %get-tuple-element.6), channel_id=1, replica_groups=mesh['section'=8,'vocab'=32] {'section'}, use_global_device_ids=true, to_apply=%region_18.19 | all-reduce | flops 256 | bytes 2048 | tf_op jit(solution)/shard_map/psum | solution.py:72
  676.2 74.8 %psum.38 = f32[96]{0:T(128)S(1)} all-reduce(f32[96]{0:T(128)S(1)} %get-tuple-element.7), channel_id=1, replica_groups=mesh['section'=8,'vocab'=32] {'vocab'}, use_global_device_ids=true, to_apply=%region_16.17 | all-reduce | flops 96 | bytes 768 | tf_op jit(solution)/shard_map/psum | solution.py:67
  751.0 1.8 convolution_convert_fusion.2
  (10 shorter events, 0.1 us)
Async XLA Ops:
  7.2 2.7 copy-start
  7.2 94.9 %copy-start.1 = (s32[2048]{0:T(1024)S(1)}, s32[2048]{0:T(1024)}, u32[]{:S(2)}) copy-start(s32[2048]{0:T(1024)} %param.10) | copy-start | bytes 24580
  7.2 214.8 %all-gather.2.cloned.1.call-start = ((), (), s32[]{:S(2)}) async-start(), calls=%async_computation.2 | async-start | bytes 12976128 | tf_op jit(solution)/shard_map/all_gather | solution.py:35
  101.5 526.0 %reduce-scatter.3.cloned.1.call-start = ((), (), s32[]{:S(2)}) async-start(), calls=%async_computation.3 | async-start | bytes 12976128 | tf_op jit(solution)/shard_map/reduce_scatter | solution.py:54
  102.1 4.5 copy-start.2
  394.9 266.6 %reduce-scatter.5.cloned.1.call-start = ((), (), s32[]{:S(2)}) async-start(), calls=%async_computation.4 | async-start | bytes 442368 | tf_op jit(solution)/shard_map/reduce_scatter | solution.py:62
  627.5 34.0 %copy-start.3 = (f32[256]{0:T(256)S(1)}, f32[256]{0:T(256)}, u32[]{:S(2)}) copy-start(f32[256]{0:T(256)} %param.7) | copy-start | bytes 3076
Sparse Core Ops, SparseCore 0:
  101.6 120.2 all-gather.1
  395.0 232.4 reduce-scatter.2
  630.0 31.4 reduce-scatter.4
where the time goes:
time: 761 us; the launch traced here: 760 us
  waiting for transfers between devices  364 us (48%)
  blocking collectives  327 us (43%)
  matrix products  37.6 us (5%)
  between operations  15.7 us (2%)
  other arithmetic  9.79 us (1%)
    reduce_scatter x1, waiting for transfers between devices, body(): lax.psum_scatter(lax.dot_general(head_weight, dlogits, (((1,), (1,)), (()...  232 us
    all_gather x1, waiting for transfers between devices, body(): full_rows = lax.all_gather(section_rows, 'vocab', axis=1, tiled=True)  110 us
    psum x1, blocking collectives, body(): squares = lax.psum(jnp.sum(rows_own * rows_own, axis=1), 'vocab')  76.2 us
    pmax x1, blocking collectives, body(): row_peak = lax.pmax(local_peak, ('section', 'vocab'))  75.4 us
    psum x1, blocking collectives, body(): inner_dots = lax.psum(jnp.sum(scaled * rows_own, axis=1), 'vocab') / D  74.8 us
    psum x1, blocking collectives, body(): lax.psum((local_total, picked_part), ('section', 'vocab'))  72.1 us
    reduce_scatter x1, waiting for transfers between devices, body(): lax.psum_scatter(grads_turned, 'section', scatter_dimension=1, tiled=True)  22.3 us
  transfers between devices with their start and end apart: 3, of which 3 were waited for; matrix products, arithmetic and copies ran while one was open for 3% of the time, Pallas kernels for 0%

commit v1 on v0

--- a/solution.py
+++ b/solution.py
@@ -64,7 +64,9 @@
     )
     d_normed = own_grads.T
     scaled = d_normed * norm_gain[None, :]
-    inner_dots = lax.psum(jnp.sum(scaled * rows_own, axis=1), "vocab") / D
+    inner_dots = (
+        lax.all_gather(jnp.sum(scaled * rows_own, axis=1), axis_name="vocab").sum(axis=0) / D
+    )
     d_rows = (
         inverse[:, None] * scaled - rows_own * (inverse * inverse * inverse * inner_dots)[:, None]
     )

time: 761 us -> 830 us (1.091)
  blocking collectives: 327 us -> 395 us
    unnamed x0 -> x1, blocking collectives: none -> 143 us
    psum x1 -> x0, blocking collectives: 74.8 us -> none  [body(): inner_dots = lax.psum(jnp.sum(scaled * rows_own, axis=1), 'vocab') / D]
where the time goes in v1:
time: 830 us; the launch traced here: 829 us
  blocking collectives  395 us (48%)
  waiting for transfers between devices  363 us (44%)
  matrix products  37.6 us (5%)
  between operations  16.3 us (2%)
  other arithmetic  9.82 us (1%)
    reduce_scatter x1, waiting for transfers between devices, body(): lax.psum_scatter(lax.dot_general(head_weight, dlogits, (((1,), (1,)), (()...  230 us
    unnamed x1, blocking collectives  143 us
    all_gather x1, waiting for transfers between devices, body(): full_rows = lax.all_gather(section_rows, 'vocab', axis=1, tiled=True)  110 us
    psum x1, blocking collectives, body(): squares = lax.psum(jnp.sum(rows_own * rows_own, axis=1), 'vocab')  76.2 us
    pmax x1, blocking collectives, body(): row_peak = lax.pmax(local_peak, ('section', 'vocab'))  75.4 us
    psum x1, blocking collectives, body(): lax.psum((local_total, picked_part), ('section', 'vocab'))  72.1 us
    reduce_scatter x1, waiting for transfers between devices, body(): lax.psum_scatter(grads_turned, 'section', scatter_dimension=1, tiled=True)  22.6 us
  transfers between devices with their start and end apart: 3, of which 3 were waited for; matrix products, arithmetic and copies ran while one was open for 3% of the time, Pallas kernels for 0%

profile of v1, /device:TPU:0, one launch (start us, length us, event | category | flops | bytes accessed | tf_op | source)
XLA Modules:
  0.0 828.9 jit_solution(13097771108199394185)
XLA Ops:
  7.2 0.0 copy-start
  7.2 0.0 copy-start.1
  7.2 0.0 all-gather.3.cloned.1.call-start
  7.2 0.7 broadcast_compare_fusion
  8.0 0.7 copy.11
  8.7 0.6 reduce-window.6
  9.2 0.2 slice_reduce_fusion
  9.5 0.1 add_bitcast_fusion
  9.6 0.3 fusion.5
  9.8 0.0 copy-done
  9.8 0.3 multiply_reduce_fusion
  10.1 76.2 %psum.28 = f32[96]{0:T(128)S(1)} all-reduce(f32[96]{0:T(128)S(1)} %get-tuple-element.25), channel_id=1, replica_groups=mesh['section'=8,'vocab'=32] {'vocab'}, use_global_device_ids=true, to_apply=%region_4.5 | all-reduce | flops 96 | bytes 768 | tf_op jit(solution)/shard_map/psum | solution.py:27
  86.3 0.8 multiply_convert_fusion
  87.1 14.4 %all_gather.12 = bf16[768,256]{1,0:T(8,128)(2,1)} all-gather(bf16[96,256]{1,0:T(8,128)(2,1)S(1)} %multiply_convert_fusion), channel_id=1, replica_groups=mesh['section'=8,'vocab'=32] {'section'}, dimensions={0}, use_global_device_ids=true | all-gather | bytes 442368 | tf_op jit(solution)/shard_map/all_gather | solution.py:30
  101.5 0.0 all-gather.3.cloned.1.call-update
  101.5 0.0 reduce-scatter.3.cloned.1.call-start
  101.5 0.2 select_reduce_fusion
  101.8 0.1 broadcast_add_fusion
  101.9 0.1 add.108
  101.9 0.1 reshape.157
  102.1 0.0 copy-done.1
  102.1 0.0 copy-start.2
  102.1 4.5 gather_fusion
  106.6 0.0 copy-done.2
  106.6 0.7 fusion.30
  107.3 4.4 fusion.23
  111.7 110.2 %all-gather.3.cloned.1.call-done = bf16[768,8192]{1,0:T(8,128)(2,1)} async-done(((bf16[768,256]{1,0:T(8,128)(2,1)}), bf16[768,8192]{1,0:T(8,128)(2,1)}) %all-gather.3.cloned.1.call-update) | async-done | bytes 12582928 | tf_op jit(solution)/shard_map/all_gather | solution.py:35
  221.9 11.3 %fusion.31 = (f32[768]{0:T(1024)S(1)}, f32[768,384]{0,1:T(8,128)S(1)}) fusion(bf16[768,8192]{1,0:T(8,128)(2,1)} %all-gather.3.cloned.1.call-done, bf16[8192,384]{1,0:T(8,128)(2,1)} %param.8), kind=kOutput, calls=%fused_computation.66 | convolution fusion | flops 4832132096 | bytes 20057088 | tf_op jit(solution)/shard_map/dot_general | solution.py:38
  233.2 75.4 %pmax.7 = f32[768]{0:T(1024)S(1)} all-reduce(f32[768]{0:T(1024)S(1)} %get-tuple-element.27), channel_id=1, replica_groups=mesh['section'=8,'vocab'=32] {'section','vocab'}, use_global_device_ids=true, to_apply=%region_6.7 | all-reduce | flops 768 | bytes 6144 | tf_op jit(solution)/shard_map/pmax | solution.py:44
  308.6 0.3 fusion.1
  308.9 72.1 %all-reduce.1 = (f32[768]{0:T(1024)S(1)}, f32[768]{0:T(1024)S(1)}) all-reduce(f32[768]{0:T(1024)S(1)} %get-tuple-element.5, f32[768]{0:T(1024)S(1)} %get-tuple-element.4), channel_id=1, replica_groups=mesh['section'=8,'vocab'=32] {'section','vocab'}, use_global_device_ids=true, to_apply=%region_8.9 | all-reduce | flops 1536 | bytes 12288 | tf_op jit(solution)/shard_map/psum | solution.py:46
  381.0 1.3 select_reduce_fusion.1
  382.3 12.6 %fusion = bf16[8192,768]{0,1:T(8,128)(2,1)} fusion(bf16[8192,384]{1,0:T(8,128)(2,1)} %param.8, f32[768,384]{0,1:T(8,128)S(1)} %get-tuple-element.28, f32[768]{0:T(1024)S(1)} %get-tuple-element.13, f32[768]{0:T(1024)S(1)} %get-tuple-element.16, s32[768]{0:T(1024)S(1)} %gather_fusion, s32[384]{0:T(512)S(1)} %iota_add_fusion), kind=kOutput, calls=%fused_computation.2 | convolution fusion | flops 4839899136 | bytes 20064768 | tf_op jit(solution)/shard_map/dot_general | solution.py:55
  394.9 0.0 reduce-scatter.3.cloned.1.call-update
  394.9 0.2 reduce-scatter.5.cloned.1.call-start
  395.1 0.4 copy-done.4
  395.6 0.6 dynamic-slice
  397.4 229.9 %reduce-scatter.3.cloned.1.call-done = bf16[256,768]{0,1:T(8,128)(2,1)} async-done(((bf16[8192,768]{0,1:T(8,128)(2,1)}), bf16[256,768]{0,1:T(8,128)(2,1)}) %reduce-scatter.3.cloned.1.call-update) | async-done | bytes 393232 | tf_op jit(solution)/shard_map/reduce_scatter | solution.py:54
  627.3 0.0 reduce-scatter.5.cloned.1.call-update
  627.4 0.0 copy-start.3
  627.4 11.7 %convolution_convert_fusion.1 = bf16[8192,384]{1,0:T(8,128)(2,1)} fusion(bf16[768,8192]{1,0:T(8,128)(2,1)} %all-gather.3.cloned.1.call-done, f32[768,384]{0,1:T(8,128)S(1)} %get-tuple-element.28, f32[768]{0:T(1024)S(1)} %get-tuple-element.13, f32[768]{0:T(1024)S(1)} %get-tuple-element.16, s32[768]{0:T(1024)S(1)} %gather_fusion, s32[384]{0:T(512)S(1)} %iota_add_fusion), kind=kOutput, calls=%fused_computation.3 | convolution fusion | flops 4836753408 | bytes 20064768 | tf_op jit(solution)/shard_map/dot_general | solution.py:51
  639.1 22.6 %reduce-scatter.5.cloned.1.call-done = bf16[256,96]{0,1:T(8,128)(2,1)} async-done(((bf16[256,768]{0,1:T(8,128)(2,1)}), bf16[256,96]{0,1:T(8,128)(2,1)}) %reduce-scatter.5.cloned.1.call-update) | async-done | bytes 49168 | tf_op jit(solution)/shard_map/reduce_scatter | solution.py:62
  661.6 1.0 fusion.12
  662.6 13.6 %psum.31 = f32[256]{0:T(256)} all-reduce(f32[256]{0:T(256)S(1)} %get-tuple-element.6), channel_id=1, replica_groups=mesh['section'=8,'vocab'=32] {'section'}, use_global_device_ids=true, to_apply=%region_18.19 | all-reduce | flops 256 | bytes 2048 | tf_op jit(solution)/shard_map/psum | solution.py:74
  676.3 0.2 dynamic-update-slice
  676.5 142.8 %all-reduce = f32[3072]{0:T(1024)S(1)} all-reduce(f32[3072]{0:T(1024)S(1)} %dynamic-update-slice), channel_id=2, replica_groups=mesh['section'=8,'vocab'=32] {'vocab'}, use_global_device_ids=true, to_apply=%add | all-reduce | flops 3072 | bytes 24576
  819.3 0.1 reshape.181
  819.4 1.8 convolution_convert_fusion.2
  (14 shorter events, 0.2 us)
Async XLA Ops:
  7.2 2.7 copy-start
  7.2 94.9 %copy-start.1 = (s32[2048]{0:T(1024)S(1)}, s32[2048]{0:T(1024)}, u32[]{:S(2)}) copy-start(s32[2048]{0:T(1024)} %param.10) | copy-start | bytes 24580
  7.2 214.8 %all-gather.3.cloned.1.call-start = ((), (), s32[]{:S(2)}) async-start(), calls=%async_computation.2 | async-start | bytes 12976128 | tf_op jit(solution)/shard_map/all_gather | solution.py:35
  101.5 525.9 %reduce-scatter.3.cloned.1.call-start = ((), (), s32[]{:S(2)}) async-start(), calls=%async_computation.3 | async-start | bytes 12976128 | tf_op jit(solution)/shard_map/reduce_scatter | solution.py:54
  102.1 4.5 copy-start.2
  394.9 0.7 copy-start.4
  394.9 266.7 %reduce-scatter.5.cloned.1.call-start = ((), (), s32[]{:S(2)}) async-start(), calls=%async_computation.4 | async-start | bytes 442368 | tf_op jit(solution)/shard_map/reduce_scatter | solution.py:62
  627.4 34.3 %copy-start.3 = (f32[256]{0:T(256)S(1)}, f32[256]{0:T(256)}, u32[]{:S(2)}) copy-start(f32[256]{0:T(256)} %param.7) | copy-start | bytes 3076
Sparse Core Ops, SparseCore 0:
  101.6 120.2 all-gather.2
  395.0 232.2 reduce-scatter.2
  629.9 31.7 reduce-scatter.4
